TPU v7x, 256 devices: a whole 4x4x8 slice. The times are simulated.
256 devices in a mesh: row: 16 (over z, core), col: 4 (over x), depth: 4 (over y).
Axes of the slice: x: 4, y: 4, z: 8, core: 2. Of those that a mesh axis runs over, the one named last changes fastest.
Arguments:
- tokens: bfloat16 [1536, 12288], P(('depth', 'col'), 'row'), may hold values from -6 to 6
- weight: bfloat16 [12288, 24576], P('row', 'col'), may hold values from -0.0546875 to 0.0546875
- cotangent: bfloat16 [1536, 24576], P(('depth', 'row'), 'col'), may hold values from -6 to 6
Outputs:
- activated: bfloat16 [1536, 24576], P(('depth', 'row'), 'col')
- grad_tokens: bfloat16 [1536, 12288], P(('depth', 'col'), 'row')
- grad_weight: bfloat16 [12288, 24576], P('row', ('col', 'depth'))
All inputs are finite; a program needn't handle non-finite values.
Results may differ from a plain program's by a relative error of at most 0.0049.
Values may be sent and summed in bfloat16 or wider, within the bound.
A program may use at most 128 MiB of HBM per device.

v0:
```python
import math

import jax
import jax.numpy as jnp
from jax import lax
from jax.sharding import PartitionSpec as P

root_coef = math.sqrt(2.0 / math.pi)
cubic_coef = 0.044715


def gelu_tanh(values):
    hyper = jnp.tanh(root_coef * (values + cubic_coef * values * values * values))
    return 0.5 * values * (1.0 + hyper)


def gelu_slope(values):
    hyper = jnp.tanh(root_coef * (values + cubic_coef * values * values * values))
    inner = root_coef * (1.0 + 3.0 * cubic_coef * values * values)
    return 0.5 * (1.0 + hyper) + 0.5 * values * (1.0 - hyper * hyper) * inner


def on_device(tokens, weight, cotangent):
    gathered = lax.all_gather(tokens, "col", axis=0, tiled=True)
    block_rows = gathered
    preact = lax.psum_scatter(
        jnp.dot(block_rows, weight, preferred_element_type=jnp.float32),
        "row",
        scatter_dimension=0,
        tiled=True,
    )
    activated = gelu_tanh(preact).astype(jnp.bfloat16)
    grad_preact = (cotangent.astype(jnp.float32) * gelu_slope(preact)).astype(jnp.bfloat16)
    grad_rows = lax.all_gather(grad_preact, "row", axis=0, tiled=True)
    block_rows = grad_rows
    grad_tokens = lax.psum_scatter(
        lax.dot_general(
            block_rows, weight, (((1,), (1,)), ((), ())), preferred_element_type=jnp.float32
        ),
        "col",
        scatter_dimension=0,
        tiled=True,
    ).astype(jnp.bfloat16)
    partial_grad = lax.dot_general(
        gathered, grad_rows, (((0,), (0,)), ((), ())), preferred_element_type=jnp.float32
    )
    grad_weight = lax.psum_scatter(partial_grad, "depth", scatter_dimension=1, tiled=True)
    return (activated, grad_tokens, grad_weight.astype(jnp.bfloat16))


def solution(mesh):
    placed = (P(("depth", "col"), "row"), P("row", "col"), P(("depth", "row"), "col"))
    return jax.shard_map(
        on_device,
        mesh=mesh,
        in_specs=placed,
        out_specs=(
            P(("depth", "row"), "col"),
            P(("depth", "col"), "row"),
            P("row", ("col", "depth")),
        ),
        check_vma=False,
    )
```

profile of v0, /device:TPU:4, one launch (start us, length us, event | category | flops | bytes accessed | tf_op | source)
XLA Modules:
  0.0 367.4 jit_solution(13824293798596105397)
XLA Ops:
  7.2 0.0 reduce-scatter.4.cloned.1.call-start
  7.2 14.0 %all_gather.6 = bf16[384,768]{1,0:T(8,128)(2,1)S(1)} all-gather(bf16[96,768]{1,0:T(8,128)(2,1)} %param.3), channel_id=1, replica_groups=mesh['row'=16,'col'=4,'depth'=4] {'col'}, dimensions={0}, use_global_device_ids=true | all-gather | bytes 737280 | tf_op jit(solution)/shard_map/all_gather | solution.py:24
  21.2 9.9 %fusion.8 = f32[384,6144]{1,0:T(8,128)} fusion(bf16[384,768]{1,0:T(8,128)(2,1)S(1)} %all_gather.6, bf16[768,6144]{1,0:T(8,128)(2,1)} %param.4), kind=kOutput, calls=%fused_computation.12 | convolution fusion | flops 3623878656 | bytes 19464192 | tf_op jit(solution)/shard_map/dot_general | solution.py:27
  31.1 0.0 copy-start
  31.1 0.0 reduce-scatter.4.cloned.1.call-update
  31.1 0.0 all-gather.2.cloned.1.call-start
  31.2 75.4 %reduce-scatter.4.cloned.1.call-done = f32[24,6144]{1,0:T(8,128)} async-done(((f32[384,6144]{1,0:T(8,128)}), f32[24,6144]{1,0:T(8,128)}) %reduce-scatter.4.cloned.1.call-update) | async-done | bytes 589840 | tf_op jit(solution)/shard_map/reduce_scatter | solution.py:26
  106.6 0.0 copy-done
  106.6 2.3 fusion.7
  108.9 0.0 all-gather.2.cloned.1.call-update
  108.9 0.0 reduce-scatter.6.cloned.1.call-start
  108.9 41.9 %all-gather.2.cloned.1.call-done = bf16[384,6144]{1,0:T(8,128)(2,1)} async-done(((bf16[24,6144]{1,0:T(8,128)(2,1)}), bf16[384,6144]{1,0:T(8,128)(2,1)}) %all-gather.2.cloned.1.call-update) | async-done | bytes 4718608 | tf_op jit(solution)/shard_map/all_gather | solution.py:34
  150.9 10.0 %fusion.9 = f32[384,768]{1,0:T(8,128)} fusion(bf16[384,6144]{1,0:T(8,128)(2,1)} %all-gather.2.cloned.1.call-done, bf16[768,6144]{1,0:T(8,128)(2,1)} %param.4), kind=kOutput, calls=%fused_computation.13 | convolution fusion | flops 3623878656 | bytes 15335424 | tf_op jit(solution)/shard_map/dot_general | solution.py:37
  160.9 0.0 reduce-scatter.6.cloned.1.call-update
  160.9 0.0 reduce-scatter.8.cloned.1.call-start
  160.9 11.5 %convolution_bitcast_fusion = f32[768,6144]{0,1:T(8,128)} fusion(bf16[384,6144]{1,0:T(8,128)(2,1)} %all-gather.2.cloned.1.call-done, bf16[384,768]{1,0:T(8,128)(2,1)S(1)} %all_gather.6), kind=kOutput, calls=%fused_computation | convolution fusion | flops 3623878656 | bytes 24182784 | tf_op jit(solution)/shard_map/dot_general | solution.py:44
  172.4 0.0 reduce-scatter.8.cloned.1.call-update
  172.5 12.2 %reduce-scatter.6.cloned.1.call-done = f32[96,768]{1,0:T(8,128)} async-done(((f32[384,768]{1,0:T(8,128)}), f32[96,768]{1,0:T(8,128)}) %reduce-scatter.6.cloned.1.call-update) | async-done | bytes 294928 | tf_op jit(solution)/shard_map/reduce_scatter | solution.py:36
  184.7 1.6 convert_element_type.18
  186.3 169.6 %reduce-scatter.8.cloned.1.call-done = f32[768,1536]{0,1:T(8,128)} async-done(((f32[768,6144]{0,1:T(8,128)}), f32[768,1536]{0,1:T(8,128)}) %reduce-scatter.8.cloned.1.call-update) | async-done | bytes 4718608 | tf_op jit(solution)/shard_map/reduce_scatter | solution.py:47
  355.9 2.6 convert_element_type.19
  358.5 2.4 copy.6
Async XLA Ops:
  7.2 99.4 %reduce-scatter.4.cloned.1.call-start = ((), (), s32[]{:S(2)}) async-start(), calls=%async_computation.3 | async-start | bytes 10027008 | tf_op jit(solution)/shard_map/reduce_scatter | solution.py:26
  31.1 75.5 %copy-start = (bf16[24,6144]{1,0:T(8,128)(2,1)S(1)}, bf16[24,6144]{1,0:T(8,128)(2,1)}, u32[]{:S(2)}) copy-start(bf16[24,6144]{1,0:T(8,128)(2,1)} %param.5) | copy-start | bytes 884740
  31.1 119.8 %all-gather.2.cloned.1.call-start = ((), (), s32[]{:S(2)}) async-start(), calls=%async_computation.4 | async-start | bytes 5013504 | tf_op jit(solution)/shard_map/all_gather | solution.py:34
  108.9 75.8 %reduce-scatter.6.cloned.1.call-start = ((), (), s32[]{:S(2)}) async-start(), calls=%async_computation.5 | async-start | bytes 1474560 | tf_op jit(solution)/shard_map/reduce_scatter | solution.py:36
  160.9 195.0 %reduce-scatter.8.cloned.1.call-start = ((), (), s32[]{:S(2)}) async-start(), calls=%async_computation.6 | async-start | bytes 23592960 | tf_op jit(solution)/shard_map/reduce_scatter | solution.py:47
Sparse Core Ops, SparseCore 0:
  31.2 75.2 reduce-scatter.3
  109.0 41.8 all-gather.1
  161.0 23.6 reduce-scatter.5
  187.2 168.6 reduce-scatter.7
where the time goes:
time: 369 us; the launch traced here: 367 us
  waiting for transfers between devices  299 us (81%)
  matrix products  31.4 us (9%)
  blocking collectives  14 us (4%)
  between operations  13.8 us (4%)
  other arithmetic  6.5 us (2%)
    reduce_scatter x1, waiting for transfers between devices, on_device(): lax.psum_scatter(partial_grad, 'depth', scatter_dimension=1, tiled=True)  170 us
    reduce_scatter x1, waiting for transfers between devices, on_device(): lax.psum_scatter(jnp.dot(block_rows, weight, preferred_element_type=jnp.f...  75.4 us
    all_gather x1, waiting for transfers between devices, on_device(): grad_rows = lax.all_gather(grad_preact, 'row', axis=0, tiled=True)  41.9 us
    all_gather x1, blocking collectives, on_device(): gathered = lax.all_gather(tokens, 'col', axis=0, tiled=True)  14 us
    reduce_scatter x1, waiting for transfers between devices, on_device(): lax.psum_scatter(lax.dot_general(block_rows, weight, (((1,), (1,)), ((),...  12.2 us
    dot_general x1, matrix products, on_device(): lax.dot_general(gathered, grad_rows, (((0,), (0,)), ((), ())), preferred_...  11.5 us
    dot_general x1, matrix products, on_device(): lax.dot_general(block_rows, weight, (((1,), (1,)), ((), ())), preferred_e...  9.98 us
    dot_general x1, matrix products, on_device(): jnp.dot(block_rows, weight, preferred_element_type=jnp.float32)  9.87 us
  transfers between devices with their start and end apart: 4, of which 4 were waited for; matrix products, arithmetic and copies ran while one was open for 4% of the time, Pallas kernels for 0%

commit v1 on v0

v1 whole, which is shorter than its diff:
```python
import functools
import math

import jax
import jax.numpy as jnp
from jax import lax
from jax.experimental import pallas as pl
from jax.experimental.pallas import tpu as pltpu
from jax.sharding import PartitionSpec as P

root_coef = math.sqrt(2.0 / math.pi)
cubic_coef = 0.044715

RING = 8
SIDE = 4
SUB = 48
HALF = 768
CHUNK = 2 * HALF
SHARE = 24
PADDED = 32
TILE = 256
f32, bf16 = jnp.float32, jnp.bfloat16


def wrap(value, extent):
    return lax.rem(value + 2 * extent, extent)


def kernel(
    tok, weight, cot, act_out, gt_out, gw_out,
    T, W, W_sib, part, hop, first, cot_send, cot_recv, act_send, act_recv,
    G, TT, GT, y_send, y_recv, x_send, x_recv, x_own,
    local_sem, send_sem, recv_sem,
):
    row, col, dep = (lax.axis_index(name) for name in ("row", "col", "depth"))
    z, k = row // 2, lax.rem(row, 2)
    tau = 1 - 2 * k

    def device(dz=0, dx=0, dy=0, flip=False):
        core = 1 - k if flip else k
        return (2 * wrap(z + dz, RING) + core, wrap(col + dx, SIDE), wrap(dep + dy, SIDE))

    sibling = device(flip=True)
    numbers = {}
    pending = []

    def number(key):
        return numbers.setdefault(key, len(numbers))

    def copy(key, source, target, to):
        n = number(key)
        return pltpu.make_async_remote_copy(
            src_ref=source, dst_ref=target, send_sem=send_sem.at[n], recv_sem=recv_sem.at[n],
            device_id=to, device_id_type=pl.DeviceIdType.MESH,
        )

    def send(key, source, target, to):
        transfer = copy(key, source, target, to)
        transfer.start()
        pending.append(transfer)

    def receive(key, slot):
        copy(key, slot, slot, sibling).wait_recv()

    local = []
    for half in range(2):
        columns = pl.ds(pl.multiple_of(dep * CHUNK + half * HALF, HALF), HALF)
        local.append(pltpu.make_async_copy(weight.at[:, columns], W.at[half], local_sem.at[half]))
    local.append(pltpu.make_async_copy(tok, T.at[0, dep, col], local_sem.at[2]))
    for transfer in local:
        transfer.start()

    partners = [device(dz=1), device(dz=-1), sibling]
    for step in range(1, SIDE):
        partners += [device(dx=step), device(dy=step), device(dy=step, flip=True)]
    barrier = pltpu.get_barrier_semaphore()
    for partner in partners:
        pl.semaphore_signal(barrier, inc=1, device_id=partner, device_id_type=pl.DeviceIdType.MESH)

    gap = jnp.zeros((PADDED - SHARE, HALF), f32)
    for piece in range(SIDE):
        for half in range(2):
            begin = piece * CHUNK + half * HALF
            values = cot[:, begin : begin + HALF].astype(f32)
            cot_send[piece, half] = jnp.concatenate([values, gap], axis=0).astype(bf16)
    pl.semaphore_wait(barrier, len(partners))

    for s in (1, -1):
        send(("xo", s), tok, T.at[0, dep, col], device(dx=s * tau))
        send(("y0", s), tok.at[0], T.at[0, dep, col, 0], device(dy=s * tau))
    send(("k0", 0), tok, T.at[1, dep, col], sibling)
    columns = pl.ds(pl.multiple_of(dep * CHUNK + (1 - k) * HALF, HALF), HALF)
    send("w", weight.at[:, columns], W_sib, sibling)

    def at_col(j):
        return wrap(col + j * tau, SIDE)

    def at_dep(j):
        return wrap(dep + j * tau, SIDE)

    def start_y1(j):
        slot = T.at[0, dep, at_col(j), 1]
        source = tok.at[1] if j == 0 else slot
        for s in (1, -1):
            send(("y1", j, s), source, slot, device(dy=s * tau))

    def relay_y1(j):
        slot = T.at[0, at_dep(-1), at_col(j), 1]
        receive(("y1", j, 1), slot)
        send(("y1r", j), slot, slot, device(dy=tau))

    def start_x0(j):
        slot = T.at[0, at_dep(j), col, 0]
        for s in (1, -1):
            send(("x0", j, s), slot, slot, device(dx=s * tau))

    def relay_x0(j):
        slot = T.at[0, at_dep(j), at_col(-1), 0]
        receive(("x0", j, 1), slot)
        send(("x0r", j), slot, slot, device(dx=tau))

    def to_sibling_block(j):
        slot = T.at[0, dep, at_col(j)]
        send(("k0", j), slot, T.at[1, dep, at_col(j)], sibling)

    start_y1(0)
    slot = T.at[0, dep, at_col(-1)]
    receive(("xo", 1), slot)
    send("xor", slot, slot, device(dx=tau))
    start_y1(-1)
    to_sibling_block(-1)
    slot = T.at[0, at_dep(-1), col, 0]
    receive(("y0", 1), slot)
    send("y0r", slot, slot, device(dy=tau))
    start_x0(-1)
    receive(("xo", -1), T.at[0, dep, at_col(1)])
    start_y1(1)
    to_sibling_block(1)
    receive(("y0", -1), T.at[0, at_dep(1), col, 0])
    start_x0(1)
    relay_y1(0)
    receive("xor", T.at[0, dep, at_col(2)])
    to_sibling_block(2)
    start_y1(2)

    steps = (0, 1, -1, 2)

    def stream(i):
        return wrap(dep + steps[i], SIDE)

    def ring(j):
        return wrap(z + j * tau, RING)

    def partial_preact(i):
        group = stream(i)

        def tile(n, carry):
            lanes = pl.ds(pl.multiple_of(n * TILE, TILE), TILE)
            own = T[0, group].reshape(RING * SUB, HALF)
            other = T[1, group].reshape(RING * SUB, HALF)
            total = jnp.dot(own, W[k, :, lanes], preferred_element_type=f32)
            total += jnp.dot(other, W_sib[:, lanes], preferred_element_type=f32)
            part[i, :, :, lanes] = total.reshape(RING, SUB, TILE)
            return carry

        lax.fori_loop(0, HALF // TILE, tile, 0)

    def enter(i):
        partial_preact(i)
        first[i, 0] = part[i, ring(4)].astype(bf16)
        send(("r", i, 0, 0), first.at[i, 0], hop.at[i, 0, 0], device(dz=tau))
        first[i, 1] = part[i, ring(-3)].astype(bf16)
        send(("r", i, 1, 1), first.at[i, 1], hop.at[i, 1, 1], device(dz=-tau))

    def pass_on(i, way, at, j):
        receive(("r", i, way, at), hop.at[i, way, at])
        hop[i, way, at] = (hop[i, way, at].astype(f32) + part[i, ring(j)]).astype(bf16)
        to = device(dz=tau if way == 0 else -tau)
        send(("r", i, way, at + 1), hop.at[i, way, at], hop.at[i, way, at + 1], to)

    def spread(i, block, ways):
        slot = G.at[block, k, stream(i)]
        for key, to in ways:
            send(key, slot, slot, to)

    def finish(i):
        receive(("r", i, 0, 3), hop.at[i, 0, 3])
        receive(("r", i, 1, 3), hop.at[i, 1, 3])
        v = part[i, z] + hop[i, 0, 3].astype(f32) + hop[i, 1, 3].astype(f32)
        group = stream(i)
        for flip in range(2):
            if i or flip:
                core = 1 - k if flip else k
                receive(("c", -steps[i] % SIDE, flip), cot_recv.at[group, core])
        hyper = jnp.tanh(root_coef * (v + cubic_coef * v * v * v))
        inner = root_coef * (1.0 + 3.0 * cubic_coef * v * v)
        slope = 0.5 * (1.0 + hyper) + 0.5 * v * (1.0 - hyper * hyper) * inner
        given = jnp.concatenate(
            [cot_recv[group, core].astype(f32)[:SHARE] for core in range(2)], axis=0
        )
        G[z, k, group] = (given * slope).astype(bf16)
        spread(i, z, [
            (("g", i, 0, 1), device(dz=tau)), (("g", i, 1, 1), device(dz=-tau)),
            (("s", i, 0), sibling),
        ])
        active = 0.5 * v * (1.0 + hyper)
        for core in range(2):
            mine = active[core * SHARE : (core + 1) * SHARE]
            act_send[group, core] = jnp.concatenate([mine, gap], axis=0).astype(bf16)
        for flip in range(2):
            core = 1 - k if flip else k
            if i == 0 and flip == 0:
                act_recv[dep, k] = act_send[dep, k]
            else:
                send(
                    ("a", steps[i] % SIDE, flip), act_send.at[group, core], act_recv.at[dep, k],
                    device(dy=steps[i], flip=bool(flip)),
                )

    def relay(i, far):
        for way in range(2):
            if way == 1 and far == 4:
                continue
            j = -far if way == 0 else far
            block = ring(j)
            receive(("g", i, way, far), G.at[block, k, stream(i)])
            ways = []
            if far < (4 if way == 0 else 3):
                ways.append((("g", i, way, far + 1), device(dz=tau if way == 0 else -tau)))
            ways.append((("s", i, j), sibling))
            spread(i, block, ways)

    def sibling_blocks():
        for j in (0, -1, 1, 2):
            receive(("k0", j), T.at[1, dep, at_col(-j)])

    for transfer in local:
        transfer.wait()
    receive("w", W_sib)
    sibling_blocks()
    enter(0)

    slot = T.at[0, at_dep(2), col, 0]
    receive("y0r", slot)
    start_x0(2)
    relay_x0(-1)
    relay_x0(1)
    relay_y1(-1)
    relay_y1(1)
    relay_x0(2)
    relay_y1(2)

    for step in range(SIDE):
        for flip in range(2):
            piece = wrap(dep + step, SIDE)
            core = 1 - k if flip else k
            if step == 0 and flip == 0:
                cot_recv[dep, k] = cot_send[dep, k]
            else:
                send(
                    ("c", step, flip), cot_send.at[piece, core], cot_recv.at[dep, k],
                    device(dy=step, flip=bool(flip)),
                )

    pass_on(0, 0, 0, 3)
    pass_on(0, 1, 1, -2)

    for j in (-1, 1):
        receive(("x0", j, -1), T.at[0, at_dep(j), at_col(1), 0])
        receive(("x0r", j), T.at[0, at_dep(j), at_col(2), 0])
    for j in (0, -1, 1, 2):
        receive(("y1", j, -1), T.at[0, at_dep(1), at_col(j), 1])
    for i in (1, 2):
        send(("k", i), T.at[0, stream(i)], T.at[1, stream(i)], sibling)
    receive(("x0", 2, -1), T.at[0, at_dep(2), at_col(1), 0])
    receive(("x0r", 2), T.at[0, at_dep(2), at_col(2), 0])
    for j in (0, -1, 1, 2):
        receive(("y1r", j), T.at[0, at_dep(2), at_col(j), 1])
    send(("k", 3), T.at[0, stream(3)], T.at[1, stream(3)], sibling)
    for i in (1, 2, 3):
        receive(("k", i), T.at[1, stream(i)])
        enter(i)

    def transpose(c):
        rows = jnp.concatenate(
            [T[0, y, c, half] for half in range(2) for y in range(SIDE)], axis=0
        )
        TT[:, c * 2 * SIDE * SUB : (c + 1) * 2 * SIDE * SUB] = rows.T

    transpose(0)
    transpose(1)
    for i in range(1, 4):
        pass_on(i, 0, 0, 3)
        pass_on(i, 1, 1, -2)
    transpose(2)
    transpose(3)
    for i in range(4):
        pass_on(i, 0, 1, 2)
        pass_on(i, 1, 2, -1)
    for i in range(4):
        pass_on(i, 0, 2, 1)
    for i in range(4):
        finish(i)

    order = (0, -1, 1, -2, 2, -3, 3, 4)

    def block_start(q):
        j = order[q]
        block = ring(j)
        for i in range(4):
            receive(("s", i, -j), G.at[block, 1 - k, stream(i)])

        def tile(n, carry):
            at = pl.multiple_of(n * TILE, TILE)
            total = jnp.zeros((SIDE * SUB, TILE), f32)
            for half in range(2):
                total += lax.dot_general(
                    G[block, half].reshape(SIDE * SUB, HALF), W[half, pl.ds(at, TILE)],
                    (((1,), (1,)), ((), ())), preferred_element_type=f32,
                )
            GT[q, :, :, pl.ds(at, TILE)] = total.reshape(SIDE, SUB, TILE)
            return carry

        lax.fori_loop(0, HALF // TILE, tile, 0)
        y_send[q, 0] = GT[q, at_dep(2)].astype(bf16)
        send(("p", q, 0), y_send.at[q, 0], y_recv.at[q, 0], device(dy=tau))
        y_send[q, 1] = GT[q, at_dep(-1)].astype(bf16)
        send(("p", q, 2), y_send.at[q, 1], y_recv.at[q, 2], device(dy=-tau))

    def block_pass(q):
        receive(("p", q, 0), y_recv.at[q, 0])
        y_recv[q, 0] = (y_recv[q, 0].astype(f32) + GT[q, at_dep(1)]).astype(bf16)
        send(("p", q, 1), y_recv.at[q, 0], y_recv.at[q, 1], device(dy=tau))

    base = number("x")
    for extra in range(1, 2 * SIDE):
        number(("x", extra))

    def x_copy(n, source, target, to):
        return pltpu.make_async_remote_copy(
            src_ref=source, dst_ref=target, send_sem=send_sem.at[base + n],
            recv_sem=recv_sem.at[base + n], device_id=to,
            device_id_type=pl.DeviceIdType.MESH,
        )

    def block_end(q):
        receive(("p", q, 1), y_recv.at[q, 1])
        receive(("p", q, 2), y_recv.at[q, 2])
        total = GT[q, dep] + y_recv[q, 1].astype(f32) + y_recv[q, 2].astype(f32)
        block = ring(order[q])
        half, home = lax.rem(block, 2), block // 2
        away = wrap(home - col, SIDE)

        @pl.when(away == 0)
        def _():
            x_own[half] = total

        @pl.when(away != 0)
        def _():
            x_send[half, away] = total.astype(bf16)
            x_copy(
                half * SIDE + away, x_send.at[half, away], x_recv.at[half, away],
                device(dx=away),
            ).start()

    def grad_weight(begin, end):
        def tile(n, carry):
            half = n // 3
            inner = pl.multiple_of(lax.rem(n, 3) * TILE, TILE)
            right = G[:, half, :, :, pl.ds(inner, TILE)].reshape(RING * SIDE * SUB, TILE)
            total = jnp.dot(TT[...], right, preferred_element_type=f32)
            gw_out[:, pl.ds(pl.multiple_of(n * TILE, TILE), TILE)] = total.astype(bf16)
            return carry

        lax.fori_loop(begin, end, tile, 0)

    for i in range(4):
        relay(i, 1)
    block_start(0)
    for i in range(4):
        relay(i, 2)
    block_pass(0)
    block_start(1)
    block_start(2)
    for i in range(4):
        relay(i, 3)
    block_end(0)
    block_pass(1)
    block_pass(2)
    block_start(3)
    block_start(4)
    for i in range(4):
        relay(i, 4)
    block_end(1)
    block_end(2)
    block_pass(3)
    block_pass(4)
    block_start(5)
    block_start(6)
    block_start(7)
    block_end(3)
    block_end(4)
    block_pass(5)
    block_pass(6)
    grad_weight(0, 2)
    block_pass(7)
    block_end(5)
    block_end(6)
    grad_weight(2, 4)
    block_end(7)
    grad_weight(4, 6)

    for step in range(SIDE):
        for flip in range(2):
            if step or flip:
                core = 1 - k if flip else k
                receive(("a", step, flip), act_recv.at[wrap(dep - step, SIDE), core])
    for piece in range(SIDE):
        for half in range(2):
            begin = piece * CHUNK + half * HALF
            act_out[:, begin : begin + HALF] = (
                act_recv[piece, half].astype(f32)[:SHARE].astype(bf16)
            )

    for half in range(2):
        total = x_own[half]
        for away in range(1, SIDE):
            slot = x_recv.at[half, away]
            x_copy(half * SIDE + away, slot, slot, sibling).wait_recv()
            total += x_recv[half, away].astype(f32)
        gt_out[half] = total.astype(bf16)
    for transfer in pending:
        transfer.wait_send()
    for half in range(2):
        for away in range(1, SIDE):
            slot = x_recv.at[half, away]
            x_copy(half * SIDE + away, slot, slot, sibling).wait_send()


def on_device(tokens, weight, cotangent):
    scratch = [
        pltpu.VMEM((2, SIDE, SIDE, 2, SUB, HALF), bf16),
        pltpu.VMEM((2, HALF, HALF), bf16),
        pltpu.VMEM((HALF, HALF), bf16),
        pltpu.VMEM((SIDE, RING, SUB, HALF), f32),
        pltpu.VMEM((SIDE, 2, 4, SUB, HALF), bf16),
        pltpu.VMEM((SIDE, 2, SUB, HALF), bf16),
        pltpu.VMEM((SIDE, 2, PADDED, HALF), bf16),
        pltpu.VMEM((SIDE, 2, PADDED, HALF), bf16),
        pltpu.VMEM((SIDE, 2, PADDED, HALF), bf16),
        pltpu.VMEM((SIDE, 2, PADDED, HALF), bf16),
        pltpu.VMEM((RING, 2, SIDE, SUB, HALF), bf16),
        pltpu.VMEM((HALF, RING * SIDE * SUB), bf16),
        pltpu.VMEM((RING, SIDE, SUB, HALF), f32),
        pltpu.VMEM((RING, 2, SUB, HALF), bf16),
        pltpu.VMEM((RING, 3, SUB, HALF), bf16),
        pltpu.VMEM((2, SIDE, SUB, HALF), bf16),
        pltpu.VMEM((2, SIDE, SUB, HALF), bf16),
        pltpu.VMEM((2, SUB, HALF), f32),
        pltpu.SemaphoreType.DMA((3,)),
        pltpu.SemaphoreType.DMA((256,)),
        pltpu.SemaphoreType.DMA((256,)),
    ]
    activated, grad_tokens, grad_weight = pl.pallas_call(
        kernel,
        out_shape=(
            jax.ShapeDtypeStruct((SHARE, SIDE * CHUNK), bf16),
            jax.ShapeDtypeStruct((2, SUB, HALF), bf16),
            jax.ShapeDtypeStruct((HALF, CHUNK), bf16),
        ),
        in_specs=[
            pl.BlockSpec(memory_space=pl.ANY),
            pl.BlockSpec(memory_space=pl.ANY),
            pl.BlockSpec(memory_space=pltpu.VMEM),
        ],
        out_specs=[pl.BlockSpec(memory_space=pltpu.VMEM)] * 3,
        scratch_shapes=scratch,
        compiler_params=pltpu.CompilerParams(
            collective_id=0, has_side_effects=True, vmem_limit_bytes=60 * 2**20
        ),
        cost_estimate=pl.CostEstimate(
            flops=11 * 10**9, bytes_accessed=8 * 10**6, transcendentals=10**5
        ),
        name="gelu_grid",
    )(tokens.reshape(2, SUB, HALF), weight, cotangent)
    return activated, grad_tokens.reshape(2 * SUB, HALF), grad_weight


def solution(mesh):
    placed = (P(("depth", "col"), "row"), P("row", "col"), P(("depth", "row"), "col"))
    return jax.shard_map(
        on_device,
        mesh=mesh,
        in_specs=placed,
        out_specs=(
            P(("depth", "row"), "col"),
            P(("depth", "col"), "row"),
            P("row", ("col", "depth")),
        ),
        check_vma=False,
    )
```

time: 369 us -> 108 us (0.29)
  waiting for transfers between devices: 299 us -> 0 us
  Pallas kernels: 0 us -> 101 us
  matrix products: 31.4 us -> 0 us
  blocking collectives: 14 us -> 0 us
  between operations: 13.8 us -> 0.64 us
  other arithmetic: 6.5 us -> 0 us
  local copies, waits for them, and re-layouts: 2.44 us -> 6.5 us
    reduce_scatter x3 -> x0, waiting for transfers between devices: 257 us -> none  [the longest x1 170 us: on_device(): lax.psum_scatter(partial_grad, 'depth', scatter_dimension=1, tiled=True)]
    pallas_call x0 -> x1, Pallas kernels: none -> 101 us  [on_device(): pl.pallas_call(kernel, out_shape=(jax.ShapeDtypeStruct((SHARE, SIDE * CHU...]
    all_gather x1 -> x0, waiting for transfers between devices: 41.9 us -> none  [on_device(): grad_rows = lax.all_gather(grad_preact, 'row', axis=0, tiled=True)]
    dot_general x3 -> x0, matrix products: 31.4 us -> none  [the longest x1 11.5 us: on_device(): lax.dot_general(gathered, grad_rows, (((0,), (0,)), ((), ())), preferred_...]
    all_gather x1 -> x0, blocking collectives: 14 us -> none  [on_device(): gathered = lax.all_gather(tokens, 'col', axis=0, tiled=True)]
    convert_element_type x3 -> x0, other arithmetic: 6.5 us -> none  [the longest x1 2.57 us: on_device(): return (activated, grad_tokens, grad_weight.astype(jnp.bfloat16))]
    unnamed x3, local copies, waits for them, and re-layouts: 2.44 us -> 6.5 us
  transfers between devices with their start and end apart: 4 -> 0, of which waited for: 4 -> 0; matrix products, arithmetic and copies ran while one was open for 4% -> 0% of each run, Pallas kernels for 0% -> 0%
where the time goes in v1:
time: 108 us
  Pallas kernels  101 us (94%)
  local copies, waits for them, and re-layouts  6.5 us (6%)
    pallas_call x1, Pallas kernels, on_device(): pl.pallas_call(kernel, out_shape=(jax.ShapeDtypeStruct((SHARE, SIDE * CHU...  101 us
    unnamed x3, local copies, waits for them, and re-layouts  6.5 us

profile of v1, /device:TPU:4, one launch (start us, length us, event | category | flops | bytes accessed | tf_op | source)
XLA Modules:
  0.0 107.6 jit_solution(15974048880416819980)
XLA Ops:
  0.6 100.5 %gelu_grid.1 = (bf16[24,6144]{1,0:T(8,128)(2,1)}, bf16[2,48,768]{2,1,0:T(8,128)(2,1)}, bf16[768,1536]{1,0:T(8,128)(2,1)}) custom-call(bf16[2,48,768]{2,1,0:T(8,128)(2,1)} %bitcast.3, bf16[768,6144]{1,0:T(8,128)(2,1)} %weight.1, bf16[24,6144]{1,0:T(8,128)(2,1)} %cot.1), custom_call_target="tpu_custom_call" | custom-call | flops 11000000512 | bytes 8000000 | tf_op jit(solution)/shard_map/gelu_grid/pallas_call | solution.py:464
  101.1 1.7 %copy.9 = bf16[24,6144]{1,0:T(8,128)(2,1)} copy(bf16[24,6144]{1,0:T(8,128)(2,1)} %get-tuple-element.12) | data formatting | bytes 589824
  102.8 1.6 %copy.10 = bf16[96,768]{1,0:T(8,128)(2,1)} copy(bf16[96,768]{1,0:T(8,128)(2,1)} %bitcast.2) | data formatting | bytes 294912
  104.4 3.2 %copy.11 = bf16[768,1536]{1,0:T(8,128)(2,1)} copy(bf16[768,1536]{1,0:T(8,128)(2,1)} %get-tuple-element.14) | data formatting | bytes 4718592

commit v2 on v0

v2 whole, which is shorter than its diff:
```python
import functools
import math

import jax
import jax.numpy as jnp
from jax import lax
from jax.experimental import pallas as pl
from jax.experimental.pallas import tpu as pltpu
from jax.sharding import PartitionSpec as P

root_coef = math.sqrt(2.0 / math.pi)
cubic_coef = 0.044715

RING = 8
SIDE = 4
SUB = 48
HALF = 768
CHUNK = 2 * HALF
SHARE = 24
PADDED = 32
TILE = 256
f32, bf16 = jnp.float32, jnp.bfloat16


def wrap(value, extent):
    return lax.rem(value + 2 * extent, extent)


PIECES = 4


def kernel(
    tok, weight, cot, act_out, gt_out, gw_out,
    T, T_sib, W, W_rest, W_sib, part, hop, first, cot_send, cot_recv, cot_both,
    act_both, act_send, act_recv, g_send, G, TT, GT, y_send, y_recv, x_send, x_recv, x_own,
    gw_tiles, cot_held, act_held, gt_held, local_sem, send_sem, recv_sem,
):
    row, col, dep = (lax.axis_index(name) for name in ("row", "col", "depth"))
    z, k = row // 2, lax.rem(row, 2)
    tau = 1 - 2 * k

    def device(dz=0, dx=0, dy=0, flip=False):
        core = 1 - k if flip else k
        return (2 * wrap(z + dz, RING) + core, wrap(col + dx, SIDE), wrap(dep + dy, SIDE))

    sibling = device(flip=True)
    numbers = {}
    groups = {}

    def number(key):
        return numbers.setdefault(key, len(numbers))

    def copy(group, key, source, target, to):
        return pltpu.make_async_remote_copy(
            src_ref=source, dst_ref=target,
            send_sem=send_sem.at[groups.setdefault(group, len(groups))],
            recv_sem=recv_sem.at[number(key)],
            device_id=to, device_id_type=pl.DeviceIdType.MESH,
        )

    def send(group, key, source, target, to):
        copy(group, key, source, target, to).start()

    def receive(key, size):
        copy("x", key, size, size, sibling).wait_recv()

    def all_sent(group, size):
        copy(group, ("x", 1), size, size, sibling).wait_send()

    def at_col(j):
        return wrap(col + j * tau, SIDE)

    def at_dep(j):
        return wrap(dep + j * tau, SIDE)

    def ring(j):
        return wrap(z + j * tau, RING)

    steps = (0, 2, 1, -1)

    def unit_group(i):
        return wrap(dep + steps[i], SIDE)

    def token_group(i):
        return wrap(dep - steps[i], SIDE)

    def lanes_of(i, half):
        return pl.ds(pl.multiple_of(unit_group(i) * CHUNK + half * HALF, HALF), HALF)

    local = [pltpu.make_async_copy(tok, T.at[dep, col], local_sem.at[0])]
    for i in range(SIDE):
        local.append(
            pltpu.make_async_copy(weight.at[:, lanes_of(i, k)], W.at[i], local_sem.at[1 + i])
        )
    local.append(pltpu.make_async_copy(weight.at[:, lanes_of(0, 1 - k)], W_rest, local_sem.at[5]))
    local.append(pltpu.make_async_copy(cot, cot_held, local_sem.at[6]))
    for transfer in local:
        transfer.start()

    partners = [device(dz=1), device(dz=-1), sibling]
    for step in range(1, SIDE):
        partners += [device(dx=step), device(dy=step)]
    barrier = pltpu.get_barrier_semaphore()
    for partner in partners:
        pl.semaphore_signal(barrier, inc=1, device_id=partner, device_id_type=pl.DeviceIdType.MESH)
    gap = jnp.zeros((PADDED - SHARE, HALF), f32)

    def padded(values):
        return jnp.concatenate([values, gap], axis=0).astype(bf16)

    pl.semaphore_wait(barrier, len(partners))

    for j in (1, -1, 2):
        send("x", ("x", j), tok, T.at[dep, col], device(dx=j * tau))
    send("k", "k", tok, T_sib.at[col], sibling)
    for i in range(SIDE):
        send("w", ("w", i), weight.at[:, lanes_of(i, 1 - k)], W_sib.at[i], sibling)
    for transfer in local:
        transfer.wait()
    for i in range(SIDE):
        cot_send[i] = padded(cot_held[:, lanes_of(i, 1 - k)].astype(f32))
        send("c", "c", cot_send.at[i], cot_recv.at[i], sibling)
    for j in (1, -1, 2):
        slot = T.at[dep, at_col(-j)]
        receive(("x", j), slot)
        send("k", "k" if j != 2 else "k2", slot, T_sib.at[at_col(-j)], sibling)
    for s in (1, -1):
        send("y", "y" if s == 1 else "ys", T.at[dep], T.at[dep], device(dy=s * tau))

    def relay_tokens():
        slot = T.at[at_dep(-1)]
        receive("y", slot)
        send("y", "ys", slot, slot, device(dy=tau))

    def partial_preact(i, columns):
        count = len(columns) * 2 * SUB

        def tile(n, carry):
            lanes = pl.ds(pl.multiple_of(n * TILE, TILE), TILE)
            own = jnp.stack([T[dep, at_col(j)] for j in columns]).reshape(count, HALF)
            other = jnp.stack([T_sib[at_col(j)] for j in columns]).reshape(count, HALF)
            total = jnp.dot(own, W[i, :, lanes], preferred_element_type=f32)
            total += jnp.dot(other, W_sib[i, :, lanes], preferred_element_type=f32)
            total = total.reshape(len(columns), 2, SUB, TILE)
            for n, j in enumerate(columns):
                part[i, at_col(j), :, :, lanes] = total[n]
            return carry

        lax.fori_loop(0, HALF // TILE, tile, 0)

    def of_block(i, block):
        return part[i, block // 2, lax.rem(block, 2)]

    def enter(i):
        first[i, 0] = of_block(i, ring(4)).astype(bf16)
        send("r", ("r", i, 1), first.at[i, 0], hop.at[i, 0], device(dz=tau))
        first[i, 1] = of_block(i, ring(-3)).astype(bf16)
        send("r", ("r", i, 1), first.at[i, 1], hop.at[i, 4], device(dz=-tau))

    def reduce_step(i, at):
        receive(("r", i, at), hop.at[i, pl.ds(0, 2 if at < 3 else 1)])
        for way in range(2 if at < 3 else 1):
            slot, j = (at - 1, 4 - at) if way == 0 else (3 + at, at - 3)
            later = 4 if slot + 1 in (3, 6) else at + 1
            hop[i, slot] = (hop[i, slot].astype(f32) + of_block(i, ring(j))).astype(bf16)
            send(
                "r", ("r", i, later), hop.at[i, slot], hop.at[i, slot + 1],
                device(dz=tau if way == 0 else -tau),
            )

    def spread(i, block, ways):
        slot = G.at[block, k, token_group(i)]
        for group, key, to in ways:
            send(group, key, slot, slot, to)

    def share(i, far):
        if far == 0:
            return ("s", 0)
        if far == 4:
            return ("s", 4, i)
        return ("s", far, (2, 0, 1, 1)[i])

    def begin(i):
        if i > 0:
            receive(("h", i), G.at[z, k, token_group(i)])
        spread(i, z, [
            ("g", ("g", i, 1), device(dz=tau)), ("g", ("g", i, 1), device(dz=-tau)),
            ("s", share(i, 0), sibling),
        ])

    def finish(i):
        receive(("r", i, 4), hop.at[i, pl.ds(0, 2)])
        v = of_block(i, z) + hop[i, 3].astype(f32) + hop[i, 6].astype(f32)
        cot_both[k] = cot_held[:, lanes_of(i, k)].astype(f32)
        cot_both[1 - k] = cot_recv[i].astype(f32)[:SHARE]
        given = cot_both[...].reshape(SUB, HALF)
        hyper = jnp.tanh(root_coef * (v + cubic_coef * v * v * v))
        inner = root_coef * (1.0 + 3.0 * cubic_coef * v * v)
        slope = 0.5 * (1.0 + hyper) + 0.5 * v * (1.0 - hyper * hyper) * inner
        gradient = (given * slope).astype(bf16)
        if i == 0:
            G[z, k, dep] = gradient
            begin(0)
        else:
            g_send[i] = gradient
            send("h", ("h", i), g_send.at[i], G.at[z, k, dep], device(dy=steps[i]))
        act_both[...] = (0.5 * v * (1.0 + hyper)).reshape(2, SHARE, HALF)
        act_held[:, lanes_of(i, k)] = act_both[k].astype(bf16)
        act_send[i] = padded(act_both[1 - k])
        send("a", "a", act_send.at[i], act_recv.at[i], sibling)

    def relay(i, far):
        receive(("g", i, far), hop.at[0, pl.ds(0, 2 if far < 4 else 1)])
        for way in range(2 if far < 4 else 1):
            ways = []
            if far < (4 if way == 0 else 3):
                ways.append(("g", ("g", i, far + 1), device(dz=tau if way == 0 else -tau)))
            ways.append(("s", share(i, far), sibling))
            spread(i, ring(-far if way == 0 else far), ways)

    def transpose(y):
        rows = T[y].reshape(RING * SUB, HALF)
        TT[:, y * RING * SUB : (y + 1) * RING * SUB] = rows.T

    def blocks(far):
        if far == 0:
            return [(0, z)]
        if far == 4:
            return [(7, ring(4))]
        return [(2 * far - 1, ring(-far)), (2 * far, ring(far))]

    def partial_tokens(far, streams):
        pieces = [(q, block, token_group(i)) for i in streams for q, block in blocks(far)]
        receive(share(streams[0], far), hop.at[0, pl.ds(0, len(pieces))])

        def tile(n, carry):
            at = pl.multiple_of(n * TILE, TILE)
            total = jnp.zeros((len(pieces) * SUB, TILE), f32)
            for half, right in ((k, W.at[0]), (1 - k, W_rest)):
                left = jnp.concatenate([G[block, half, group] for q, block, group in pieces], axis=0)
                total += lax.dot_general(
                    left, right[pl.ds(at, TILE)], (((1,), (1,)), ((), ())),
                    preferred_element_type=f32,
                )
            for m, (q, block, group) in enumerate(pieces):
                GT[q, group, :, pl.ds(at, TILE)] = total[m * SUB : (m + 1) * SUB]
            return carry

        lax.fori_loop(0, HALF // TILE, tile, 0)

    def send_piece(far, key, q, n, j, to):
        y_send[q, n] = GT[q, at_dep(j)].astype(bf16)
        send("p", key, y_send.at[q, n], y_recv.at[q, n], device(dy=to * tau))

    def stage_far_row(far):
        for q, block in blocks(far):
            send_piece(far, ("p", far, 0), q, 0, 2, 1)

    def stage_near_row(far):
        for q, block in blocks(far):
            send_piece(far, ("p", far, 1), q, 2, -1, -1)

    def block_one(far):
        partial_tokens(far, (1,))
        stage_far_row(far)

    def block_two(far):
        partial_tokens(far, (2, 3))
        stage_near_row(far)

    def block_pass(far):
        receive(("p", far, 0), hop.at[0, pl.ds(0, len(blocks(far)))])
        for q, block in blocks(far):
            y_recv[q, 0] = (y_recv[q, 0].astype(f32) + GT[q, at_dep(1)]).astype(bf16)
            send("p", ("p", far, 1), y_recv.at[q, 0], y_recv.at[q, 1], device(dy=tau))

    def last_block(i):
        partial_tokens(4, (i,))
        if i > 0:
            y_send[7, i - 1] = GT[7, token_group(i)].astype(bf16)
            send(
                "p", ("p", 4), y_send.at[7, i - 1], y_recv.at[7, i - 1], device(dy=-steps[i])
            )

    def block_end(far):
        key = ("p", 4) if far == 4 else ("p", far, 1)
        receive(key, hop.at[0, pl.ds(0, 3 if far == 4 else 2 * len(blocks(far)))])
        for q, block in blocks(far):
            total = GT[q, dep]
            for n in range(0 if far == 4 else 1, 3):
                total += y_recv[q, n].astype(f32)
            half, home = lax.rem(block, 2), block // 2
            away = wrap(home - col, SIDE)

            @pl.when(away == 0)
            def _():
                x_own[half] = total

            @pl.when(away != 0)
            def _():
                x_send[half, away - 1] = total.astype(bf16)
                send(
                    "home", "home", x_send.at[half, away - 1], x_recv.at[half, away - 1],
                    device(dx=away),
                )

    def write_tile(n):
        return pltpu.make_async_copy(
            gw_tiles.at[n], gw_out.at[:, pl.ds(pl.multiple_of(n * TILE, TILE), TILE)],
            local_sem.at[n],
        )

    def grad_weight(begin, end):
        def tile(n, carry):
            half = n // 3
            inner = pl.multiple_of(lax.rem(n, 3) * TILE, TILE)
            right = jnp.concatenate(
                [G[:, half, y, :, pl.ds(inner, TILE)].reshape(RING * SUB, TILE) for y in range(4)],
                axis=0,
            )
            gw_tiles[n] = jnp.dot(TT[...], right, preferred_element_type=f32).astype(bf16)
            write_tile(n).start()
            return carry

        lax.fori_loop(begin, end, tile, 0)

    write_act = pltpu.make_async_copy(act_held, act_out, local_sem.at[6])
    write_gt = pltpu.make_async_copy(gt_held, gt_out, local_sem.at[7])

    def activations():
        receive("a", act_recv)
        for i in range(SIDE):
            act_held[:, lanes_of(i, 1 - k)] = act_recv[i].astype(f32)[:SHARE].astype(bf16)
        write_act.start()

    turns = (1, 2, 3, 0)

    receive("k", T.at[0, pl.ds(0, 3)])
    receive(("w", turns[0]), W_sib.at[turns[0]])
    partial_preact(turns[0], (0, 1, -1))
    receive("k2", T.at[0, 0])
    partial_preact(turns[0], (2,))
    enter(turns[0])
    for i in turns[1:]:
        receive(("w", i), W_sib.at[i])
        partial_preact(i, (0, 1, -1, 2))
        enter(i)
    for i in turns:
        reduce_step(i, 1)
    relay_tokens()
    for at in (2, 3):
        for i in turns:
            reduce_step(i, at)
    receive("c", cot_recv)
    for i in turns:
        finish(i)
    for i in (1, 2, 3):
        begin(i)
    receive("ys", T.at[pl.ds(0, 2)])
    partial_tokens(0, (0, 1, 2, 3))
    stage_far_row(0)
    stage_near_row(0)
    for far in (1, 2, 3):
        relay(1, far)
        block_pass(far - 1)
        if far > 1:
            partial_tokens(far - 1, (0,))
        relay(2, far)
        block_one(far)
        relay(3, far)
        if far == 1:
            transpose(0)
            transpose(1)
        if far == 2:
            transpose(2)
            transpose(3)
        if far == 3:
            activations()
        relay(0, far)
        block_two(far)
        block_end(far - 1)
    relay(1, 4)
    block_pass(3)
    relay(2, 4)
    last_block(1)
    relay(3, 4)
    last_block(2)
    relay(0, 4)
    last_block(3)
    partial_tokens(3, (0,))
    last_block(0)
    grad_weight(0, 1)
    block_end(3)
    grad_weight(1, 3)
    block_end(4)
    grad_weight(3, 6)

    receive("home", hop.at[0, pl.ds(0, 6)])
    for half in range(2):
        total = x_own[half]
        for n in range(SIDE - 1):
            total += x_recv[half, n].astype(f32)
        gt_held[half] = total.astype(bf16)
    write_gt.start()
    for group, size in (
        ("x", T.at[0, pl.ds(0, 3)]), ("k", T.at[0]), ("w", W_sib), ("c", cot_recv),
        ("y", T.at[pl.ds(0, 3)]), ("r", hop), ("h", g_send.at[pl.ds(0, 3)]), ("g", hop),
        ("s", G.at[pl.ds(0, 4)]), ("a", act_recv), ("p", y_recv), ("home", x_send),
    ):
        all_sent(group, size)
    for n in range(CHUNK // TILE):
        write_tile(n).wait()
    write_act.wait()
    write_gt.wait()


def deliver(act, gt, gw, act_out, gt_out, gw_out, act_held, gt_held, gw_held, sem):
    moves = [(act, act_held, act_out), (gt, gt_held, gt_out)]
    for n in range(PIECES):
        rows = pl.ds(n * (HALF // PIECES), HALF // PIECES)
        moves.append((gw.at[rows], gw_held.at[rows], gw_out.at[rows]))
    into = [
        pltpu.make_async_copy(source, held, sem.at[0, n])
        for n, (source, held, target) in enumerate(moves)
    ]
    out_of = [
        pltpu.make_async_copy(held, target, sem.at[1, n])
        for n, (source, held, target) in enumerate(moves)
    ]
    for move in into:
        move.start()
    for arrived, move in zip(into, out_of):
        arrived.wait()
        move.start()
    for move in out_of:
        move.wait()


def on_device(tokens, weight, cotangent):
    scratch = [
        pltpu.VMEM((SIDE, SIDE, 2, SUB, HALF), bf16),
        pltpu.VMEM((SIDE, 2, SUB, HALF), bf16),
        pltpu.VMEM((SIDE, HALF, HALF), bf16),
        pltpu.VMEM((HALF, HALF), bf16),
        pltpu.VMEM((SIDE, HALF, HALF), bf16),
        pltpu.VMEM((SIDE, SIDE, 2, SUB, HALF), f32),
        pltpu.VMEM((SIDE, 7, SUB, HALF), bf16),
        pltpu.VMEM((SIDE, 2, SUB, HALF), bf16),
        pltpu.VMEM((SIDE, PADDED, HALF), bf16),
        pltpu.VMEM((SIDE, PADDED, HALF), bf16),
        pltpu.VMEM((2, SHARE, HALF), f32),
        pltpu.VMEM((2, SHARE, HALF), f32),
        pltpu.VMEM((SIDE, PADDED, HALF), bf16),
        pltpu.VMEM((SIDE, PADDED, HALF), bf16),
        pltpu.VMEM((SIDE, SUB, HALF), bf16),
        pltpu.VMEM((RING, 2, SIDE, SUB, HALF), bf16),
        pltpu.VMEM((HALF, RING * SIDE * SUB), bf16),
        pltpu.VMEM((RING, SIDE, SUB, HALF), f32),
        pltpu.VMEM((RING, 3, SUB, HALF), bf16),
        pltpu.VMEM((RING, 3, SUB, HALF), bf16),
        pltpu.VMEM((2, SIDE - 1, SUB, HALF), bf16),
        pltpu.VMEM((2, SIDE - 1, SUB, HALF), bf16),
        pltpu.VMEM((2, SUB, HALF), f32),
        pltpu.VMEM((CHUNK // TILE, HALF, TILE), bf16),
        pltpu.VMEM((SHARE, SIDE * CHUNK), bf16),
        pltpu.VMEM((SHARE, SIDE * CHUNK), bf16),
        pltpu.VMEM((2, SUB, HALF), bf16),
        pltpu.SemaphoreType.DMA((8,)),
        pltpu.SemaphoreType.DMA((12,)),
        pltpu.SemaphoreType.DMA((72,)),
    ]
    out_shape = (
        jax.ShapeDtypeStruct((SHARE, SIDE * CHUNK), bf16),
        jax.ShapeDtypeStruct((2, SUB, HALF), bf16),
        jax.ShapeDtypeStruct((HALF, CHUNK), bf16),
    )
    anywhere = pl.BlockSpec(memory_space=pl.ANY)
    results = pl.pallas_call(
        kernel,
        out_shape=out_shape,
        in_specs=[anywhere] * 3,
        out_specs=[anywhere] * 3,
        scratch_shapes=scratch,
        compiler_params=pltpu.CompilerParams(
            collective_id=0, has_side_effects=True, vmem_limit_bytes=60 * 2**20
        ),
        cost_estimate=pl.CostEstimate(
            flops=11 * 10**9, bytes_accessed=15 * 10**6, transcendentals=10**5
        ),
        name="gelu_grid",
    )(tokens.reshape(2, SUB, HALF), weight, cotangent)
    activated, grad_tokens, grad_weight = pl.pallas_call(
        deliver,
        out_shape=out_shape,
        in_specs=[anywhere] * 3,
        out_specs=[anywhere] * 3,
        scratch_shapes=[pltpu.VMEM(shape.shape, bf16) for shape in out_shape]
        + [pltpu.SemaphoreType.DMA((2, PIECES + 2))],
        name="deliver",
    )(*results)
    return activated, grad_tokens.reshape(2 * SUB, HALF), grad_weight


def solution(mesh):
    placed = (P(("depth", "col"), "row"), P("row", "col"), P(("depth", "row"), "col"))
    return jax.shard_map(
        on_device,
        mesh=mesh,
        in_specs=placed,
        out_specs=(
            P(("depth", "row"), "col"),
            P(("depth", "col"), "row"),
            P("row", ("col", "depth")),
        ),
        check_vma=False,
    )
```

time: 369 us -> 89.2 us (0.24)
  waiting for transfers between devices: 299 us -> 0 us
  Pallas kernels: 0 us -> 88.2 us
  matrix products: 31.4 us -> 0 us
  blocking collectives: 14 us -> 0 us
  between operations: 13.8 us -> 0.64 us
  other arithmetic: 6.5 us -> 0 us
    reduce_scatter x3 -> x0, waiting for transfers between devices: 257 us -> none  [the longest x1 170 us: on_device(): lax.psum_scatter(partial_grad, 'depth', scatter_dimension=1, tiled=True)]
    pallas_call x0 -> x2, Pallas kernels: none -> 88.2 us  [the longest x1 85.5 us: on_device(): pl.pallas_call(kernel, out_shape=out_shape, in_specs=[anywhere] * 3, out_...]
    all_gather x1 -> x0, waiting for transfers between devices: 41.9 us -> none  [on_device(): grad_rows = lax.all_gather(grad_preact, 'row', axis=0, tiled=True)]
    dot_general x3 -> x0, matrix products: 31.4 us -> none  [the longest x1 11.5 us: on_device(): lax.dot_general(gathered, grad_rows, (((0,), (0,)), ((), ())), preferred_...]
    all_gather x1 -> x0, blocking collectives: 14 us -> none  [on_device(): gathered = lax.all_gather(tokens, 'col', axis=0, tiled=True)]
    convert_element_type x3 -> x0, other arithmetic: 6.5 us -> none  [the longest x1 2.57 us: on_device(): return (activated, grad_tokens, grad_weight.astype(jnp.bfloat16))]
  transfers between devices with their start and end apart: 4 -> 0, of which waited for: 4 -> 0; matrix products, arithmetic and copies ran while one was open for 4% -> 0% of each run, Pallas kernels for 0% -> 0%
where the time goes in v2:
time: 89.2 us; the launch traced here: 88.9 us
  Pallas kernels  88.2 us (99%)
    pallas_call x1, Pallas kernels, on_device(): pl.pallas_call(kernel, out_shape=out_shape, in_specs=[anywhere] * 3, out_...  85.5 us
    pallas_call x1, Pallas kernels, on_device(): pl.pallas_call(deliver, out_shape=out_shape, in_specs=[anywhere] * 3, out...  2.73 us

profile of v2, /device:TPU:4, one launch (start us, length us, event | category | flops | bytes accessed | tf_op | source)
XLA Modules:
  0.0 88.9 jit_solution(9601184293612015090)
XLA Ops:
  0.6 85.5 %gelu_grid.1 = (bf16[24,6144]{1,0:T(8,128)(2,1)}, bf16[2,48,768]{2,1,0:T(8,128)(2,1)}, bf16[768,1536]{1,0:T(8,128)(2,1)}) custom-call(bf16[2,48,768]{2,1,0:T(8,128)(2,1)} %bitcast.2, bf16[768,6144]{1,0:T(8,128)(2,1)} %weight.1, bf16[24,6144]{1,0:T(8,128)(2,1)} %cot.1), custom_call_target="tpu_custom_call" | custom-call | flops 11000000512 | bytes 15000000 | tf_op jit(solution)/shard_map/gelu_grid/pallas_call | solution.py:478
  86.1 2.7 %deliver.1 = (bf16[24,6144]{1,0:T(8,128)(2,1)}, bf16[2,48,768]{2,1,0:T(8,128)(2,1)}, bf16[768,1536]{1,0:T(8,128)(2,1)}) custom-call(bf16[24,6144]{1,0:T(8,128)(2,1)} %get-tuple-element.9.act, bf16[2,48,768]{2,1,0:T(8,128)(2,1)} %get-tuple-element.10.gt, bf16[768,1536]{1,0:T(8,128)(2,1)} %get-tuple-element.11.gw), custom_call_target="tpu_custom_call" | custom-call | tf_op jit(solution)/shard_map/deliver/pallas_call | solution.py:492

commit v3 on v2

--- a/solution.py
+++ b/solution.py
@@ -26,7 +26,7 @@
     return lax.rem(value + 2 * extent, extent)
 
 
-PIECES = 4
+PIECES = 8
 
 
 def kernel(
@@ -345,14 +345,15 @@
         receive(("w", i), W_sib.at[i])
         partial_preact(i, (0, 1, -1, 2))
         enter(i)
-    for i in turns:
-        reduce_step(i, 1)
+    for i, at in ((1, 1), (2, 1), (3, 1), (1, 2), (0, 1)):
+        reduce_step(i, at)
     relay_tokens()
-    for at in (2, 3):
-        for i in turns:
-            reduce_step(i, at)
+    for i, at in ((2, 2), (3, 2), (1, 3), (0, 2), (2, 3), (3, 3)):
+        reduce_step(i, at)
     receive("c", cot_recv)
-    for i in turns:
+    finish(1)
+    reduce_step(0, 3)
+    for i in (2, 3, 0):
         finish(i)
     for i in (1, 2, 3):
         begin(i)
@@ -362,12 +363,14 @@
     stage_near_row(0)
     for far in (1, 2, 3):
         relay(1, far)
+        if far > 1:
+            relay(0, far - 1)
         block_pass(far - 1)
-        if far > 1:
-            partial_tokens(far - 1, (0,))
         relay(2, far)
         block_one(far)
         relay(3, far)
+        if far > 1:
+            partial_tokens(far - 1, (0,))
         if far == 1:
             transpose(0)
             transpose(1)
@@ -376,24 +379,23 @@
             transpose(3)
         if far == 3:
             activations()
-        relay(0, far)
         block_two(far)
         block_end(far - 1)
     relay(1, 4)
+    relay(0, 3)
     block_pass(3)
     relay(2, 4)
     last_block(1)
     relay(3, 4)
     last_block(2)
-    relay(0, 4)
     last_block(3)
     partial_tokens(3, (0,))
+    relay(0, 4)
+    block_end(3)
     last_block(0)
-    grad_weight(0, 1)
-    block_end(3)
-    grad_weight(1, 3)
+    grad_weight(0, 2)
     block_end(4)
-    grad_weight(3, 6)
+    grad_weight(2, 6)
 
     receive("home", hop.at[0, pl.ds(0, 6)])
     for half in range(2):

time: 89.2 us -> 88 us (0.987)
  Pallas kernels: 88.2 us -> 86.5 us
    pallas_call x1, Pallas kernels: 85.5 us -> 83.8 us  [on_device(): pl.pallas_call(kernel, out_shape=out_shape, in_specs=[anywhere] * 3, out_...]
where the time goes in v3:
time: 88 us; the launch traced here: 87.2 us
  Pallas kernels  86.5 us (98%)
    pallas_call x1, Pallas kernels, on_device(): pl.pallas_call(kernel, out_shape=out_shape, in_specs=[anywhere] * 3, out_...  83.8 us
    pallas_call x1, Pallas kernels, on_device(): pl.pallas_call(deliver, out_shape=out_shape, in_specs=[anywhere] * 3, out...  2.69 us

profile of v3, /device:TPU:4, one launch (start us, length us, event | category | flops | bytes accessed | tf_op | source)
XLA Modules:
  0.0 87.2 jit_solution(15298909067013106408)
XLA Ops:
  0.6 83.8 %gelu_grid.1 = (bf16[24,6144]{1,0:T(8,128)(2,1)}, bf16[2,48,768]{2,1,0:T(8,128)(2,1)}, bf16[768,1536]{1,0:T(8,128)(2,1)}) custom-call(bf16[2,48,768]{2,1,0:T(8,128)(2,1)} %bitcast.2, bf16[768,6144]{1,0:T(8,128)(2,1)} %weight.1, bf16[24,6144]{1,0:T(8,128)(2,1)} %cot.1), custom_call_target="tpu_custom_call" | custom-call | flops 11000000512 | bytes 15000000 | tf_op jit(solution)/shard_map/gelu_grid/pallas_call | solution.py:480
  84.5 2.7 %deliver.1 = (bf16[24,6144]{1,0:T(8,128)(2,1)}, bf16[2,48,768]{2,1,0:T(8,128)(2,1)}, bf16[768,1536]{1,0:T(8,128)(2,1)}) custom-call(bf16[24,6144]{1,0:T(8,128)(2,1)} %get-tuple-element.9.act, bf16[2,48,768]{2,1,0:T(8,128)(2,1)} %get-tuple-element.10.gt, bf16[768,1536]{1,0:T(8,128)(2,1)} %get-tuple-element.11.gw), custom_call_target="tpu_custom_call" | custom-call | tf_op jit(solution)/shard_map/deliver/pallas_call | solution.py:494

commit v4 on v3

--- a/solution.py
+++ b/solution.py
@@ -176,8 +176,6 @@
     def share(i, far):
         if far == 0:
             return ("s", 0)
-        if far == 4:
-            return ("s", 4, i)
         return ("s", far, (2, 0, 1, 1)[i])
 
     def begin(i):
@@ -274,20 +272,11 @@
             y_recv[q, 0] = (y_recv[q, 0].astype(f32) + GT[q, at_dep(1)]).astype(bf16)
             send("p", ("p", far, 1), y_recv.at[q, 0], y_recv.at[q, 1], device(dy=tau))
 
-    def last_block(i):
-        partial_tokens(4, (i,))
-        if i > 0:
-            y_send[7, i - 1] = GT[7, token_group(i)].astype(bf16)
-            send(
-                "p", ("p", 4), y_send.at[7, i - 1], y_recv.at[7, i - 1], device(dy=-steps[i])
-            )
-
     def block_end(far):
-        key = ("p", 4) if far == 4 else ("p", far, 1)
-        receive(key, hop.at[0, pl.ds(0, 3 if far == 4 else 2 * len(blocks(far)))])
+        receive(("p", far, 1), hop.at[0, pl.ds(0, 2 * len(blocks(far)))])
         for q, block in blocks(far):
             total = GT[q, dep]
-            for n in range(0 if far == 4 else 1, 3):
+            for n in (1, 2):
                 total += y_recv[q, n].astype(f32)
             half, home = lax.rem(block, 2), block // 2
             away = wrap(home - col, SIDE)
@@ -385,14 +374,14 @@
     relay(0, 3)
     block_pass(3)
     relay(2, 4)
-    last_block(1)
+    block_one(4)
     relay(3, 4)
-    last_block(2)
-    last_block(3)
     partial_tokens(3, (0,))
+    block_two(4)
     relay(0, 4)
     block_end(3)
-    last_block(0)
+    block_pass(4)
+    partial_tokens(4, (0,))
     grad_weight(0, 2)
     block_end(4)
     grad_weight(2, 6)

time: 88 us -> 87 us (0.989)
  no operation moved by 1% of the time
where the time goes in v4:
time: 87 us; the launch traced here: 86.7 us
  Pallas kernels  86.1 us (99%)
    pallas_call x1, Pallas kernels, on_device(): pl.pallas_call(kernel, out_shape=out_shape, in_specs=[anywhere] * 3, out_...  83.4 us
    pallas_call x1, Pallas kernels, on_device(): pl.pallas_call(deliver, out_shape=out_shape, in_specs=[anywhere] * 3, out...  2.69 us

profile of v4, /device:TPU:4, one launch (start us, length us, event | category | flops | bytes accessed | tf_op | source)
XLA Modules:
  0.0 86.7 jit_solution(4468276106100199096)
XLA Ops:
  0.6 83.4 %gelu_grid.1 = (bf16[24,6144]{1,0:T(8,128)(2,1)}, bf16[2,48,768]{2,1,0:T(8,128)(2,1)}, bf16[768,1536]{1,0:T(8,128)(2,1)}) custom-call(bf16[2,48,768]{2,1,0:T(8,128)(2,1)} %bitcast.2, bf16[768,6144]{1,0:T(8,128)(2,1)} %weight.1, bf16[24,6144]{1,0:T(8,128)(2,1)} %cot.1), custom_call_target="tpu_custom_call" | custom-call | flops 11000000512 | bytes 15000000 | tf_op jit(solution)/shard_map/gelu_grid/pallas_call | solution.py:469
  84.0 2.7 %deliver.1 = (bf16[24,6144]{1,0:T(8,128)(2,1)}, bf16[2,48,768]{2,1,0:T(8,128)(2,1)}, bf16[768,1536]{1,0:T(8,128)(2,1)}) custom-call(bf16[24,6144]{1,0:T(8,128)(2,1)} %get-tuple-element.9.act, bf16[2,48,768]{2,1,0:T(8,128)(2,1)} %get-tuple-element.10.gt, bf16[768,1536]{1,0:T(8,128)(2,1)} %get-tuple-element.11.gw), custom_call_target="tpu_custom_call" | custom-call | tf_op jit(solution)/shard_map/deliver/pallas_call | solution.py:483

commit v5 on v4

--- a/solution.py
+++ b/solution.py
@@ -33,7 +33,7 @@
     tok, weight, cot, act_out, gt_out, gw_out,
     T, T_sib, W, W_rest, W_sib, part, hop, first, cot_send, cot_recv, cot_both,
     act_both, act_send, act_recv, g_send, G, TT, GT, y_send, y_recv, x_send, x_recv, x_own,
-    gw_tiles, cot_held, act_held, gt_held, local_sem, send_sem, recv_sem,
+    gw_tiles, act_held, gt_held, local_sem, send_sem, recv_sem,
 ):
     row, col, dep = (lax.axis_index(name) for name in ("row", "col", "depth"))
     z, k = row // 2, lax.rem(row, 2)
@@ -93,7 +93,6 @@
             pltpu.make_async_copy(weight.at[:, lanes_of(i, k)], W.at[i], local_sem.at[1 + i])
         )
     local.append(pltpu.make_async_copy(weight.at[:, lanes_of(0, 1 - k)], W_rest, local_sem.at[5]))
-    local.append(pltpu.make_async_copy(cot, cot_held, local_sem.at[6]))
     for transfer in local:
         transfer.start()
 
@@ -118,7 +117,7 @@
     for transfer in local:
         transfer.wait()
     for i in range(SIDE):
-        cot_send[i] = padded(cot_held[:, lanes_of(i, 1 - k)].astype(f32))
+        cot_send[i] = padded(cot[:, lanes_of(i, 1 - k)].astype(f32))
         send("c", "c", cot_send.at[i], cot_recv.at[i], sibling)
     for j in (1, -1, 2):
         slot = T.at[dep, at_col(-j)]
@@ -189,7 +188,7 @@
     def finish(i):
         receive(("r", i, 4), hop.at[i, pl.ds(0, 2)])
         v = of_block(i, z) + hop[i, 3].astype(f32) + hop[i, 6].astype(f32)
-        cot_both[k] = cot_held[:, lanes_of(i, k)].astype(f32)
+        cot_both[k] = cot[:, lanes_of(i, k)].astype(f32)
         cot_both[1 - k] = cot_recv[i].astype(f32)[:SHARE]
         given = cot_both[...].reshape(SUB, HALF)
         hyper = jnp.tanh(root_coef * (v + cubic_coef * v * v * v))
@@ -203,7 +202,7 @@
             g_send[i] = gradient
             send("h", ("h", i), g_send.at[i], G.at[z, k, dep], device(dy=steps[i]))
         act_both[...] = (0.5 * v * (1.0 + hyper)).reshape(2, SHARE, HALF)
-        act_held[:, lanes_of(i, k)] = act_both[k].astype(bf16)
+        act_held[:, lanes_of(i, k)] = act_both[k]
         act_send[i] = padded(act_both[1 - k])
         send("a", "a", act_send.at[i], act_recv.at[i], sibling)
 
@@ -319,7 +318,7 @@
     def activations():
         receive("a", act_recv)
         for i in range(SIDE):
-            act_held[:, lanes_of(i, 1 - k)] = act_recv[i].astype(f32)[:SHARE].astype(bf16)
+            act_held[:, lanes_of(i, 1 - k)] = act_recv[i].astype(f32)[:SHARE]
         write_act.start()
 
     turns = (1, 2, 3, 0)
@@ -406,7 +405,8 @@
 
 
 def deliver(act, gt, gw, act_out, gt_out, gw_out, act_held, gt_held, gw_held, sem):
-    moves = [(act, act_held, act_out), (gt, gt_held, gt_out)]
+    arriving = pltpu.make_async_copy(act, act_held, sem.at[0, PIECES + 1])
+    moves = [(gt, gt_held, gt_out)]
     for n in range(PIECES):
         rows = pl.ds(n * (HALF // PIECES), HALF // PIECES)
         moves.append((gw.at[rows], gw_held.at[rows], gw_out.at[rows]))
@@ -420,7 +420,11 @@
     ]
     for move in into:
         move.start()
-    for arrived, move in zip(into, out_of):
+    arriving.start()
+    for n, (arrived, move) in enumerate(zip(into, out_of)):
+        if n == PIECES // 2:
+            arriving.wait()
+            act_out[...] = act_held[...].astype(bf16)
         arrived.wait()
         move.start()
     for move in out_of:
@@ -453,8 +457,7 @@
         pltpu.VMEM((2, SIDE - 1, SUB, HALF), bf16),
         pltpu.VMEM((2, SUB, HALF), f32),
         pltpu.VMEM((CHUNK // TILE, HALF, TILE), bf16),
-        pltpu.VMEM((SHARE, SIDE * CHUNK), bf16),
-        pltpu.VMEM((SHARE, SIDE * CHUNK), bf16),
+        pltpu.VMEM((SHARE, SIDE * CHUNK), f32),
         pltpu.VMEM((2, SUB, HALF), bf16),
         pltpu.SemaphoreType.DMA((8,)),
         pltpu.SemaphoreType.DMA((12,)),
@@ -465,11 +468,13 @@
         jax.ShapeDtypeStruct((2, SUB, HALF), bf16),
         jax.ShapeDtypeStruct((HALF, CHUNK), bf16),
     )
+    held_act = jax.ShapeDtypeStruct((SHARE, SIDE * CHUNK), f32)
     anywhere = pl.BlockSpec(memory_space=pl.ANY)
+    inside = pl.BlockSpec(memory_space=pltpu.VMEM)
     results = pl.pallas_call(
         kernel,
-        out_shape=out_shape,
-        in_specs=[anywhere] * 3,
+        out_shape=(held_act,) + out_shape[1:],
+        in_specs=[anywhere, anywhere, inside],
         out_specs=[anywhere] * 3,
         scratch_shapes=scratch,
         compiler_params=pltpu.CompilerParams(
@@ -484,8 +489,10 @@
         deliver,
         out_shape=out_shape,
         in_specs=[anywhere] * 3,
-        out_specs=[anywhere] * 3,
-        scratch_shapes=[pltpu.VMEM(shape.shape, bf16) for shape in out_shape]
+        out_specs=[inside, anywhere, anywhere],
+        scratch_shapes=[
+            pltpu.VMEM(shape.shape, shape.dtype) for shape in (held_act,) + out_shape[1:]
+        ]
         + [pltpu.SemaphoreType.DMA((2, PIECES + 2))],
         name="deliver",
     )(*results)

time: 87 us -> 89.2 us (1.025)
  Pallas kernels: 86.1 us -> 88.2 us
    pallas_call x1, Pallas kernels: 2.69 us -> 3.93 us  [on_device(): pl.pallas_call(deliver, out_shape=out_shape, in_specs=[anywhere] * 3, out...]
where the time goes in v5:
time: 89.2 us; the launch traced here: 88.8 us
  Pallas kernels  88.2 us (99%)
    pallas_call x1, Pallas kernels, on_device(): pl.pallas_call(kernel, out_shape=(held_act,) + out_shape[1:], in_specs=[a...  84.2 us
    pallas_call x1, Pallas kernels, on_device(): pl.pallas_call(deliver, out_shape=out_shape, in_specs=[anywhere] * 3, out...  3.93 us

profile of v5, /device:TPU:4, one launch (start us, length us, event | category | flops | bytes accessed | tf_op | source)
XLA Modules:
  0.0 88.8 jit_solution(12154589620004596993)
XLA Ops:
  0.6 84.2 %gelu_grid.1 = (f32[24,6144]{1,0:T(8,128)}, bf16[2,48,768]{2,1,0:T(8,128)(2,1)}, bf16[768,1536]{1,0:T(8,128)(2,1)}) custom-call(bf16[2,48,768]{2,1,0:T(8,128)(2,1)} %bitcast.2, bf16[768,6144]{1,0:T(8,128)(2,1)} %weight.1, bf16[24,6144]{1,0:T(8,128)(2,1)} %cot.1), custom_call_target="tpu_custom_call" | custom-call | flops 11000000512 | bytes 15000000 | tf_op jit(solution)/shard_map/gelu_grid/pallas_call | solution.py:474
  84.9 3.9 %deliver.1 = (bf16[24,6144]{1,0:T(8,128)(2,1)}, bf16[2,48,768]{2,1,0:T(8,128)(2,1)}, bf16[768,1536]{1,0:T(8,128)(2,1)}) custom-call(f32[24,6144]{1,0:T(8,128)} %get-tuple-element.9.act, bf16[2,48,768]{2,1,0:T(8,128)(2,1)} %get-tuple-element.10.gt, bf16[768,1536]{1,0:T(8,128)(2,1)} %get-tuple-element.11.gw), custom_call_target="tpu_custom_call" | custom-call | tf_op jit(solution)/shard_map/deliver/pallas_call | solution.py:488
